TPU v7x, 128 devices: a whole 4x4x4 slice. The times are simulated.
128 devices in a mesh: segment: 4 (over z_lo, core), lon: 8 (over z_hi, y), lat: 4 (over x).
Axes of the slice: x: 4, y: 4, z: 4 (z_hi: 2, z_lo: 2; z = z_hi * 2 + z_lo), core: 2. Of those that a mesh axis runs over, the one named last changes fastest.
Arguments:
- latents: bfloat16 [4, 2, 24, 192, 512], P(None, None, 'lat', 'lon'), may hold values from -6 to 6
- segment_depth: int32 [4], replicated, may hold values from 1 to 2, as said below
- shift_flags: int32 [8, 2], P('segment'), may hold values from 0 to 1
- w_qkv: bfloat16 [8, 512, 1536], P('segment'), may hold values from -0.25 to 0.25
- w_out: bfloat16 [8, 512, 512], P('segment'), may hold values from -0.25 to 0.25
- w_up: bfloat16 [8, 512, 2048], P('segment'), may hold values from -0.25 to 0.25
- w_down: bfloat16 [8, 2048, 512], P('segment'), may hold values from -0.125 to 0.125
- gains: float32 [8, 2, 512], P('segment'), may hold values from 0.25 to 1.75
- logit_scale: float32 [8, 8], P('segment'), may hold values from 2 to 100
Outputs:
- sections: float32 [4, 4, 2, 24, 192, 512], P('segment', None, None, 'lat', 'lon')
Inputs may be any that keep to these rules, and one draw needn't show every extreme that they name: `segment_depth`: at least one section applies 2 layers and at least one applies a single layer.
All inputs are finite; a program needn't handle non-finite values.
Results may differ from a plain program's by a relative error of at most 0.035.
The roundings to bfloat16 on the way count: a program that leaves them out, or rounds other values in their place, can miss the bound.
Values may be sent and summed in bfloat16 or wider, within the bound.
A program may use at most 192 MiB of HBM per device.

v0:
```python
import jax
import jax.numpy as jnp
from jax import lax
from jax.sharding import PartitionSpec as P

W_LAT = 6
W_LON = 12


def extended(cells, sides, width):
    for axis, dim in sides:
        count = lax.axis_size(axis)
        head = lax.slice_in_dim(cells, 0, width, axis=dim)
        tail = lax.slice_in_dim(cells, cells.shape[dim] - width, cells.shape[dim], axis=dim)
        cells = jnp.concatenate(
            [
                lax.ppermute(tail, axis, [(i, (i + 1) % count) for i in range(count)]),
                cells,
                lax.ppermute(head, axis, [((i + 1) % count, i) for i in range(count)]),
            ],
            axis=dim,
        )
    return cells


def passed_along(value, axis, steps):
    count = lax.axis_size(axis)
    leading, last = (max(0, -steps), min(count, count - steps))
    return lax.ppermute(value, axis, [(source, source + steps) for source in range(leading, last)])


def unit_heads(block):
    return block * lax.rsqrt(jnp.sum(block * block, axis=-1, keepdims=True) + 1e-06)


def layer_norm(values, gain):
    mean = jnp.mean(values, axis=-1, keepdims=True)
    centred = values - mean
    var = jnp.mean(centred * centred, axis=-1, keepdims=True)
    return centred * lax.rsqrt(var + 1e-05) * gain


def shards(latents, segment_depth, shift_flags, w_qkv, w_out, w_up, w_down, gains, logit_scale):
    segment_idx = lax.axis_index("segment")
    segments = lax.axis_size("segment")
    lat_idx = lax.axis_index("lat")
    lat_count = lax.axis_size("lat")
    micro = latents.shape[0]
    levels, clat, clon, width = latents.shape[1:]
    heads = logit_scale.shape[1]
    head_size = width // heads
    half_lat = W_LAT // 2
    half_lon = W_LON // 2
    ext_lat = clat + W_LAT
    ext_lon = clon + W_LON
    wins = ext_lat // W_LAT * (ext_lon // W_LON)
    tokens = levels * W_LAT * W_LON
    depth = segment_depth[segment_idx]
    carry = jnp.zeros(latents.shape[1:], jnp.float32)
    sections = jnp.zeros((1, micro) + latents.shape[1:], jnp.float32)
    for tick in range(micro + segments - 1):
        inject = latents[min(tick, micro - 1)].astype(jnp.float32)
        state = jnp.where(segment_idx == 0, inject, carry)
        run_state = state
        for inner in range(w_qkv.shape[0]):
            flags = shift_flags[inner]
            rounded = run_state.astype(jnp.bfloat16)
            shape = rounded.shape
            proj = jnp.dot(
                rounded.reshape(-1, width), w_qkv[inner], preferred_element_type=jnp.float32
            )
            proj = proj.reshape(-1, 3, heads, head_size)
            query = unit_heads(proj[:, 0]).astype(jnp.bfloat16)
            keys = unit_heads(proj[:, 1]).astype(jnp.bfloat16)
            values = proj[:, 2].astype(jnp.bfloat16)
            packed = jnp.stack([query, keys, values], axis=1)
            wide = extended(
                packed.reshape(shape[:3] + (3 * width,)), (("lon", 2), ("lat", 1)), half_lon
            )
            layer_packed = wide[:, half_lon - half_lat : half_lon + clat + half_lat]
            rows = lat_idx * clat + jnp.arange(ext_lat, dtype=jnp.int32) - half_lat
            valid = (rows >= 0) & (rows < clat * lat_count)
            a_lat = (flags[0] * half_lat + half_lat) % W_LAT
            a_lon = (flags[1] * half_lon + half_lon) % W_LON
            layer_packed = jnp.roll(layer_packed, (-a_lat, -a_lon), axis=(1, 2))
            valid = jnp.roll(valid, -a_lat)
            valid = jnp.broadcast_to(valid[None, :, None], (levels, ext_lat, ext_lon))
            shaped = layer_packed.reshape(
                levels, ext_lat // W_LAT, W_LAT, ext_lon // W_LON, W_LON, 3, heads, head_size
            )
            shaped = shaped.transpose(1, 3, 0, 2, 4, 5, 6, 7).reshape(
                wins, tokens, 3, heads, head_size
            )
            keep = valid.reshape(levels, ext_lat // W_LAT, W_LAT, ext_lon // W_LON, W_LON)
            keep = keep.transpose(1, 3, 0, 2, 4).reshape(wins, tokens)
            scores = jnp.einsum(
                "wqhd,wkhd->whqk",
                shaped[:, :, 0],
                shaped[:, :, 1],
                preferred_element_type=jnp.float32,
            )
            scores = scores * logit_scale[inner][None, :, None, None]
            scores = jnp.where(keep[:, None, None, :], scores, -1e30)
            top = jnp.max(scores, axis=-1, keepdims=True)
            expo = jnp.exp(scores - top)
            weights = (expo / jnp.sum(expo, axis=-1, keepdims=True)).astype(jnp.bfloat16)
            mixed = jnp.einsum(
                "whqk,wkhd->wqhd", weights, shaped[:, :, 2], preferred_element_type=jnp.float32
            ).astype(jnp.bfloat16)
            mixed = mixed.reshape(ext_lat // W_LAT, ext_lon // W_LON, levels, W_LAT, W_LON, width)
            mixed = mixed.transpose(2, 0, 3, 1, 4, 5).reshape(levels, ext_lat, ext_lon, width)
            mixed = jnp.roll(mixed, (a_lat, a_lon), axis=(1, 2))
            mixed = mixed[:, half_lat : half_lat + clat, half_lon : half_lon + clon]
            out = jnp.dot(
                mixed.reshape(-1, width), w_out[inner], preferred_element_type=jnp.float32
            )
            gain = gains[inner]
            flat = run_state.reshape(-1, width)
            first = flat + layer_norm(out, gain[0])
            hidden = jax.nn.gelu(
                jnp.dot(first.astype(jnp.bfloat16), w_up[inner], preferred_element_type=jnp.float32)
            ).astype(jnp.bfloat16)
            down = jnp.dot(hidden, w_down[inner], preferred_element_type=jnp.float32)
            second = first + layer_norm(down, gain[1])
            fresh = second.reshape(levels, clat, clon, width)
            run_state = jnp.where(inner < depth, fresh, run_state)
        state = run_state
        which = tick - segment_idx
        placed = lax.dynamic_update_slice_in_dim(
            sections, state[None, None], jnp.clip(which, 0, micro - 1), 1
        )
        sections = jnp.where((which >= 0) & (which < micro), placed, sections)
        if tick < micro + segments - 2:
            carry = passed_along(state.astype(jnp.bfloat16), "segment", 1).astype(state.dtype)
    return sections


def solution(mesh):
    placed = (
        P(None, None, "lat", "lon", None),
        P(),
        P("segment", None),
        P("segment", None, None),
        P("segment", None, None),
        P("segment", None, None),
        P("segment", None, None),
        P("segment", None, None),
        P("segment", None),
    )
    return jax.shard_map(
        shards,
        mesh=mesh,
        in_specs=placed,
        out_specs=P("segment", None, None, "lat", "lon", None),
        check_vma=False,
    )
```

profile of v0, /device:TPU:0, one launch (start us, length us, event | category | flops | bytes accessed | tf_op | source)
XLA Modules:
  0.0 1788.3 jit_solution(3951128515917198256)
XLA Ops:
  38.9 21.5 %collective-permute-done.3 = bf16[2,6,36,1536]{3,0,2,1:T(2,128)(2,1)} collective-permute-done((bf16[2,6,36,1536]{3,0,2,1:T(2,128)(2,1)}, bf16[2,6,36,1536]{3,0,2,1:T(2,128)(2,1)}, u32[]{:S(2)}, u32[]{:S(2)}) %collective-permute-start.3) | collective-permute-done | bytes 1327136 | tf_op jit(solution)/shard_map/ppermute | solution.py:19
  74.3 9.3 reshape.1098
  163.4 24.9 %collective-permute-done.7 = bf16[2,6,36,1536]{3,0,2,1:T(2,128)(2,1)} collective-permute-done((bf16[2,6,36,1536]{3,0,2,1:T(2,128)(2,1)}, bf16[2,6,36,1536]{3,0,2,1:T(2,128)(2,1)}, u32[]{:S(2)}, u32[]{:S(2)}) %collective-permute-start.7) | collective-permute-done | bytes 1327136 | tf_op jit(solution)/shard_map/ppermute | solution.py:19
  202.1 9.3 reshape.1104
  290.7 28.3 %collective-permute-done.12 = bf16[2,6,36,1536]{3,0,2,1:T(2,128)(2,1)S(1)} collective-permute-done((bf16[2,6,36,1536]{3,0,2,1:T(2,128)(2,1)S(1)}, bf16[2,6,36,1536]{3,0,2,1:T(2,128)(2,1)S(1)}, u32[]{:S(2)}, u32[]{:S(2)}) %collective-permute-start.12) | collective-permute-done | bytes 1327136 | tf_op jit(solution)/shard_map/ppermute | solution.py:19
  332.0 9.3 reshape.1116
  407.7 7.6 collective-permute-done.13
  420.9 29.1 %collective-permute-done.16 = bf16[2,6,36,1536]{3,0,2,1:T(2,128)(2,1)S(1)} collective-permute-done((bf16[2,6,36,1536]{3,0,2,1:T(2,128)(2,1)S(1)}, bf16[2,6,36,1536]{3,0,2,1:T(2,128)(2,1)S(1)}, u32[]{:S(2)}, u32[]{:S(2)}) %collective-permute-start.16) | collective-permute-done | bytes 1327136 | tf_op jit(solution)/shard_map/ppermute | solution.py:19
  460.5 9.3 reshape.1125
  550.8 29.6 %collective-permute-done.21 = bf16[2,6,36,1536]{3,0,2,1:T(2,128)(2,1)S(1)} collective-permute-done((bf16[2,6,36,1536]{3,0,2,1:T(2,128)(2,1)S(1)}, bf16[2,6,36,1536]{3,0,2,1:T(2,128)(2,1)S(1)}, u32[]{:S(2)}, u32[]{:S(2)}) %collective-permute-start.21) | collective-permute-done | bytes 1327136 | tf_op jit(solution)/shard_map/ppermute | solution.py:19
  591.6 9.3 reshape.1134
  680.1 28.6 %collective-permute-done.25 = bf16[2,6,36,1536]{3,0,2,1:T(2,128)(2,1)S(1)} collective-permute-done((bf16[2,6,36,1536]{3,0,2,1:T(2,128)(2,1)S(1)}, bf16[2,6,36,1536]{3,0,2,1:T(2,128)(2,1)S(1)}, u32[]{:S(2)}, u32[]{:S(2)}) %collective-permute-start.25) | collective-permute-done | bytes 1327136 | tf_op jit(solution)/shard_map/ppermute | solution.py:19
  719.3 9.3 reshape.1143
  810.2 29.6 %collective-permute-done.30 = bf16[2,6,36,1536]{3,0,2,1:T(2,128)(2,1)S(1)} collective-permute-done((bf16[2,6,36,1536]{3,0,2,1:T(2,128)(2,1)S(1)}, bf16[2,6,36,1536]{3,0,2,1:T(2,128)(2,1)S(1)}, u32[]{:S(2)}, u32[]{:S(2)}) %collective-permute-start.30) | collective-permute-done | bytes 1327136 | tf_op jit(solution)/shard_map/ppermute | solution.py:19
  850.8 9.3 reshape.1152
  938.2 27.9 %collective-permute-done.34 = bf16[2,6,36,1536]{3,0,2,1:T(2,128)(2,1)S(1)} collective-permute-done((bf16[2,6,36,1536]{3,0,2,1:T(2,128)(2,1)S(1)}, bf16[2,6,36,1536]{3,0,2,1:T(2,128)(2,1)S(1)}, u32[]{:S(2)}, u32[]{:S(2)}) %collective-permute-start.34) | collective-permute-done | bytes 1327136 | tf_op jit(solution)/shard_map/ppermute | solution.py:19
  977.5 9.3 reshape.1161
  1056.3 7.7 collective-permute-done.36
  1069.1 29.1 %collective-permute-done.39 = bf16[2,6,36,1536]{3,0,2,1:T(2,128)(2,1)S(1)} collective-permute-done((bf16[2,6,36,1536]{3,0,2,1:T(2,128)(2,1)S(1)}, bf16[2,6,36,1536]{3,0,2,1:T(2,128)(2,1)S(1)}, u32[]{:S(2)}, u32[]{:S(2)}) %collective-permute-start.39) | collective-permute-done | bytes 1327136 | tf_op jit(solution)/shard_map/ppermute | solution.py:19
  1109.2 9.3 reshape.1170
  1196.1 27.3 %collective-permute-done.43 = bf16[2,6,36,1536]{3,0,2,1:T(2,128)(2,1)S(1)} collective-permute-done((bf16[2,6,36,1536]{3,0,2,1:T(2,128)(2,1)S(1)}, bf16[2,6,36,1536]{3,0,2,1:T(2,128)(2,1)S(1)}, u32[]{:S(2)}, u32[]{:S(2)}) %collective-permute-start.43) | collective-permute-done | bytes 1327136 | tf_op jit(solution)/shard_map/ppermute | solution.py:19
  1234.7 9.3 reshape.1179
  1313.5 7.4 collective-permute-done.45
  1326.0 28.8 %collective-permute-done.48 = bf16[2,6,36,1536]{3,0,2,1:T(2,128)(2,1)S(1)} collective-permute-done((bf16[2,6,36,1536]{3,0,2,1:T(2,128)(2,1)S(1)}, bf16[2,6,36,1536]{3,0,2,1:T(2,128)(2,1)S(1)}, u32[]{:S(2)}, u32[]{:S(2)}) %collective-permute-start.48) | collective-permute-done | bytes 1327136 | tf_op jit(solution)/shard_map/ppermute | solution.py:19
  1366.3 9.3 reshape.1188
  1452.8 26.9 %collective-permute-done.52 = bf16[2,6,36,1536]{3,0,2,1:T(2,128)(2,1)S(1)} collective-permute-done((bf16[2,6,36,1536]{3,0,2,1:T(2,128)(2,1)S(1)}, bf16[2,6,36,1536]{3,0,2,1:T(2,128)(2,1)S(1)}, u32[]{:S(2)}, u32[]{:S(2)}) %collective-permute-start.52) | collective-permute-done | bytes 1327136 | tf_op jit(solution)/shard_map/ppermute | solution.py:19
  1490.9 9.3 reshape.1197
  1565.6 7.2 collective-permute-done.54
  1577.8 28.9 %collective-permute-done.57 = bf16[2,6,36,1536]{3,0,2,1:T(2,128)(2,1)} collective-permute-done((bf16[2,6,36,1536]{3,0,2,1:T(2,128)(2,1)}, bf16[2,6,36,1536]{3,0,2,1:T(2,128)(2,1)}, u32[]{:S(2)}, u32[]{:S(2)}) %collective-permute-start.57) | collective-permute-done | bytes 1327136 | tf_op jit(solution)/shard_map/ppermute | solution.py:19
  1619.1 9.3 reshape.1206
  1700.4 24.6 %collective-permute-done.61 = bf16[2,6,36,1536]{3,0,2,1:T(2,128)(2,1)S(1)} collective-permute-done((bf16[2,6,36,1536]{3,0,2,1:T(2,128)(2,1)S(1)}, bf16[2,6,36,1536]{3,0,2,1:T(2,128)(2,1)S(1)}, u32[]{:S(2)}, u32[]{:S(2)}) %collective-permute-start.61) | collective-permute-done | bytes 1327136 | tf_op jit(solution)/shard_map/ppermute | solution.py:19
  1736.8 9.3 reshape.1215
  (925 shorter events, 1235.6 us)
Async XLA Ops:
  12.9 13.5 collective-permute-start
  29.3 31.0 %collective-permute-start.3 = (bf16[2,6,36,1536]{3,0,2,1:T(2,128)(2,1)}, bf16[2,6,36,1536]{3,0,2,1:T(2,128)(2,1)}, u32[]{:S(2)}, u32[]{:S(2)}) collective-permute-start(bf16[2,6,36,1536]{3,0,2,1:T(2,128)(2,1)} %copy.298), channel_id=1, source_target_pairs={{1,0},{2,1},{3,2},{0,3},{5,4},{6,5},{7,6},{4,7},{9,8},{10,9},{11,1... | collective-permute-start | bytes 3981320 | tf_op jit(solution)/shard_map/ppermute | solution.py:19
  32.2 31.6 %collective-permute-start.2 = (bf16[2,6,36,1536]{3,0,2,1:T(2,128)(2,1)}, bf16[2,6,36,1536]{3,0,2,1:T(2,128)(2,1)}, u32[]{:S(2)}, u32[]{:S(2)}) collective-permute-start(bf16[2,6,36,1536]{3,0,2,1:T(2,128)(2,1)} %copy.298), channel_id=1, source_target_pairs={{0,1},{1,2},{2,3},{3,0},{4,5},{5,6},{6,7},{7,4},{8,9},{9,10},{10,1... | collective-permute-start | bytes 3981320 | tf_op jit(solution)/shard_map/ppermute | solution.py:17
  159.4 28.9 %collective-permute-start.7 = (bf16[2,6,36,1536]{3,0,2,1:T(2,128)(2,1)}, bf16[2,6,36,1536]{3,0,2,1:T(2,128)(2,1)}, u32[]{:S(2)}, u32[]{:S(2)}) collective-permute-start(bf16[2,6,36,1536]{3,0,2,1:T(2,128)(2,1)} %copy.313), channel_id=1, source_target_pairs={{1,0},{2,1},{3,2},{0,3},{5,4},{6,5},{7,6},{4,7},{9,8},{10,9},{11,1... | collective-permute-start | bytes 3981320 | tf_op jit(solution)/shard_map/ppermute | solution.py:19
  161.8 29.7 %collective-permute-start.6 = (bf16[2,6,36,1536]{3,0,2,1:T(2,128)(2,1)}, bf16[2,6,36,1536]{3,0,2,1:T(2,128)(2,1)}, u32[]{:S(2)}, u32[]{:S(2)}) collective-permute-start(bf16[2,6,36,1536]{3,0,2,1:T(2,128)(2,1)} %copy.313), channel_id=1, source_target_pairs={{0,1},{1,2},{2,3},{3,0},{4,5},{5,6},{6,7},{7,4},{8,9},{9,10},{10,1... | collective-permute-start | bytes 3981320 | tf_op jit(solution)/shard_map/ppermute | solution.py:17
  288.6 30.4 %collective-permute-start.12 = (bf16[2,6,36,1536]{3,0,2,1:T(2,128)(2,1)S(1)}, bf16[2,6,36,1536]{3,0,2,1:T(2,128)(2,1)S(1)}, u32[]{:S(2)}, u32[]{:S(2)}) collective-permute-start(bf16[2,6,36,1536]{3,0,2,1:T(2,128)(2,1)S(1)} %copy.327), channel_id=1, source_target_pairs={{1,0},{2,1},{3,2},{0,3},{5,4},{6,5},{7,6},{4,7},{9,8},{10,9},{11,1... | collective-permute-start | bytes 3981320 | tf_op jit(solution)/shard_map/ppermute | solution.py:19
  290.4 31.9 %collective-permute-start.11 = (bf16[2,6,36,1536]{3,0,2,1:T(2,128)(2,1)S(1)}, bf16[2,6,36,1536]{3,0,2,1:T(2,128)(2,1)S(1)}, u32[]{:S(2)}, u32[]{:S(2)}) collective-permute-start(bf16[2,6,36,1536]{3,0,2,1:T(2,128)(2,1)S(1)} %copy.327), channel_id=1, source_target_pairs={{0,1},{1,2},{2,3},{3,0},{4,5},{5,6},{6,7},{7,4},{8,9},{9,10},{10,1... | collective-permute-start | bytes 3981320 | tf_op jit(solution)/shard_map/ppermute | solution.py:17
  401.5 13.8 collective-permute-start.13
  401.6 13.8 collective-permute-start.14
  418.4 31.6 %collective-permute-start.16 = (bf16[2,6,36,1536]{3,0,2,1:T(2,128)(2,1)S(1)}, bf16[2,6,36,1536]{3,0,2,1:T(2,128)(2,1)S(1)}, u32[]{:S(2)}, u32[]{:S(2)}) collective-permute-start(bf16[2,6,36,1536]{3,0,2,1:T(2,128)(2,1)S(1)} %copy.341), channel_id=1, source_target_pairs={{1,0},{2,1},{3,2},{0,3},{5,4},{6,5},{7,6},{4,7},{9,8},{10,9},{11,1... | collective-permute-start | bytes 3981320 | tf_op jit(solution)/shard_map/ppermute | solution.py:19
  418.8 32.4 %collective-permute-start.15 = (bf16[2,6,36,1536]{3,0,2,1:T(2,128)(2,1)S(1)}, bf16[2,6,36,1536]{3,0,2,1:T(2,128)(2,1)S(1)}, u32[]{:S(2)}, u32[]{:S(2)}) collective-permute-start(bf16[2,6,36,1536]{3,0,2,1:T(2,128)(2,1)S(1)} %copy.341), channel_id=1, source_target_pairs={{0,1},{1,2},{2,3},{3,0},{4,5},{5,6},{6,7},{7,4},{8,9},{9,10},{10,1... | collective-permute-start | bytes 3981320 | tf_op jit(solution)/shard_map/ppermute | solution.py:17
  548.7 31.7 %collective-permute-start.21 = (bf16[2,6,36,1536]{3,0,2,1:T(2,128)(2,1)S(1)}, bf16[2,6,36,1536]{3,0,2,1:T(2,128)(2,1)S(1)}, u32[]{:S(2)}, u32[]{:S(2)}) collective-permute-start(bf16[2,6,36,1536]{3,0,2,1:T(2,128)(2,1)S(1)} %copy.355), channel_id=1, source_target_pairs={{1,0},{2,1},{3,2},{0,3},{5,4},{6,5},{7,6},{4,7},{9,8},{10,9},{11,1... | collective-permute-start | bytes 3981320 | tf_op jit(solution)/shard_map/ppermute | solution.py:19
  549.1 32.9 %collective-permute-start.20 = (bf16[2,6,36,1536]{3,0,2,1:T(2,128)(2,1)S(1)}, bf16[2,6,36,1536]{3,0,2,1:T(2,128)(2,1)S(1)}, u32[]{:S(2)}, u32[]{:S(2)}) collective-permute-start(bf16[2,6,36,1536]{3,0,2,1:T(2,128)(2,1)S(1)} %copy.355), channel_id=1, source_target_pairs={{0,1},{1,2},{2,3},{3,0},{4,5},{5,6},{6,7},{7,4},{8,9},{9,10},{10,1... | collective-permute-start | bytes 3981320 | tf_op jit(solution)/shard_map/ppermute | solution.py:17
  661.1 13.4 collective-permute-start.22
  677.6 31.1 %collective-permute-start.25 = (bf16[2,6,36,1536]{3,0,2,1:T(2,128)(2,1)S(1)}, bf16[2,6,36,1536]{3,0,2,1:T(2,128)(2,1)S(1)}, u32[]{:S(2)}, u32[]{:S(2)}) collective-permute-start(bf16[2,6,36,1536]{3,0,2,1:T(2,128)(2,1)S(1)} %copy.369), channel_id=1, source_target_pairs={{1,0},{2,1},{3,2},{0,3},{5,4},{6,5},{7,6},{4,7},{9,8},{10,9},{11,1... | collective-permute-start | bytes 3981320 | tf_op jit(solution)/shard_map/ppermute | solution.py:19
  678.1 31.9 %collective-permute-start.24 = (bf16[2,6,36,1536]{3,0,2,1:T(2,128)(2,1)S(1)}, bf16[2,6,36,1536]{3,0,2,1:T(2,128)(2,1)S(1)}, u32[]{:S(2)}, u32[]{:S(2)}) collective-permute-start(bf16[2,6,36,1536]{3,0,2,1:T(2,128)(2,1)S(1)} %copy.369), channel_id=1, source_target_pairs={{0,1},{1,2},{2,3},{3,0},{4,5},{5,6},{6,7},{7,4},{8,9},{9,10},{10,1... | collective-permute-start | bytes 3981320 | tf_op jit(solution)/shard_map/ppermute | solution.py:17
  808.1 31.7 %collective-permute-start.30 = (bf16[2,6,36,1536]{3,0,2,1:T(2,128)(2,1)S(1)}, bf16[2,6,36,1536]{3,0,2,1:T(2,128)(2,1)S(1)}, u32[]{:S(2)}, u32[]{:S(2)}) collective-permute-start(bf16[2,6,36,1536]{3,0,2,1:T(2,128)(2,1)S(1)} %copy.383), channel_id=1, source_target_pairs={{1,0},{2,1},{3,2},{0,3},{5,4},{6,5},{7,6},{4,7},{9,8},{10,9},{11,1... | collective-permute-start | bytes 3981320 | tf_op jit(solution)/shard_map/ppermute | solution.py:19
  808.3 32.9 %collective-permute-start.29 = (bf16[2,6,36,1536]{3,0,2,1:T(2,128)(2,1)S(1)}, bf16[2,6,36,1536]{3,0,2,1:T(2,128)(2,1)S(1)}, u32[]{:S(2)}, u32[]{:S(2)}) collective-permute-start(bf16[2,6,36,1536]{3,0,2,1:T(2,128)(2,1)S(1)} %copy.383), channel_id=1, source_target_pairs={{0,1},{1,2},{2,3},{3,0},{4,5},{5,6},{6,7},{7,4},{8,9},{9,10},{10,1... | collective-permute-start | bytes 3981320 | tf_op jit(solution)/shard_map/ppermute | solution.py:17
  935.7 30.4 %collective-permute-start.34 = (bf16[2,6,36,1536]{3,0,2,1:T(2,128)(2,1)S(1)}, bf16[2,6,36,1536]{3,0,2,1:T(2,128)(2,1)S(1)}, u32[]{:S(2)}, u32[]{:S(2)}) collective-permute-start(bf16[2,6,36,1536]{3,0,2,1:T(2,128)(2,1)S(1)} %copy.397), channel_id=1, source_target_pairs={{1,0},{2,1},{3,2},{0,3},{5,4},{6,5},{7,6},{4,7},{9,8},{10,9},{11,1... | collective-permute-start | bytes 3981320 | tf_op jit(solution)/shard_map/ppermute | solution.py:19
  937.0 31.2 %collective-permute-start.33 = (bf16[2,6,36,1536]{3,0,2,1:T(2,128)(2,1)S(1)}, bf16[2,6,36,1536]{3,0,2,1:T(2,128)(2,1)S(1)}, u32[]{:S(2)}, u32[]{:S(2)}) collective-permute-start(bf16[2,6,36,1536]{3,0,2,1:T(2,128)(2,1)S(1)} %copy.397), channel_id=1, source_target_pairs={{0,1},{1,2},{2,3},{3,0},{4,5},{5,6},{6,7},{7,4},{8,9},{9,10},{10,1... | collective-permute-start | bytes 3981320 | tf_op jit(solution)/shard_map/ppermute | solution.py:17
  1067.0 31.2 %collective-permute-start.39 = (bf16[2,6,36,1536]{3,0,2,1:T(2,128)(2,1)S(1)}, bf16[2,6,36,1536]{3,0,2,1:T(2,128)(2,1)S(1)}, u32[]{:S(2)}, u32[]{:S(2)}) collective-permute-start(bf16[2,6,36,1536]{3,0,2,1:T(2,128)(2,1)S(1)} %copy.411), channel_id=1, source_target_pairs={{1,0},{2,1},{3,2},{0,3},{5,4},{6,5},{7,6},{4,7},{9,8},{10,9},{11,1... | collective-permute-start | bytes 3981320 | tf_op jit(solution)/shard_map/ppermute | solution.py:19
  1067.3 32.2 %collective-permute-start.38 = (bf16[2,6,36,1536]{3,0,2,1:T(2,128)(2,1)S(1)}, bf16[2,6,36,1536]{3,0,2,1:T(2,128)(2,1)S(1)}, u32[]{:S(2)}, u32[]{:S(2)}) collective-permute-start(bf16[2,6,36,1536]{3,0,2,1:T(2,128)(2,1)S(1)} %copy.411), channel_id=1, source_target_pairs={{0,1},{1,2},{2,3},{3,0},{4,5},{5,6},{6,7},{7,4},{8,9},{9,10},{10,1... | collective-permute-start | bytes 3981320 | tf_op jit(solution)/shard_map/ppermute | solution.py:17
  1193.6 29.8 %collective-permute-start.43 = (bf16[2,6,36,1536]{3,0,2,1:T(2,128)(2,1)S(1)}, bf16[2,6,36,1536]{3,0,2,1:T(2,128)(2,1)S(1)}, u32[]{:S(2)}, u32[]{:S(2)}) collective-permute-start(bf16[2,6,36,1536]{3,0,2,1:T(2,128)(2,1)S(1)} %copy.425), channel_id=1, source_target_pairs={{1,0},{2,1},{3,2},{0,3},{5,4},{6,5},{7,6},{4,7},{9,8},{10,9},{11,1... | collective-permute-start | bytes 3981320 | tf_op jit(solution)/shard_map/ppermute | solution.py:19
  1194.8 30.6 %collective-permute-start.42 = (bf16[2,6,36,1536]{3,0,2,1:T(2,128)(2,1)S(1)}, bf16[2,6,36,1536]{3,0,2,1:T(2,128)(2,1)S(1)}, u32[]{:S(2)}, u32[]{:S(2)}) collective-permute-start(bf16[2,6,36,1536]{3,0,2,1:T(2,128)(2,1)S(1)} %copy.425), channel_id=1, source_target_pairs={{0,1},{1,2},{2,3},{3,0},{4,5},{5,6},{6,7},{7,4},{8,9},{9,10},{10,1... | collective-permute-start | bytes 3981320 | tf_op jit(solution)/shard_map/ppermute | solution.py:17
  1323.9 30.9 %collective-permute-start.48 = (bf16[2,6,36,1536]{3,0,2,1:T(2,128)(2,1)S(1)}, bf16[2,6,36,1536]{3,0,2,1:T(2,128)(2,1)S(1)}, u32[]{:S(2)}, u32[]{:S(2)}) collective-permute-start(bf16[2,6,36,1536]{3,0,2,1:T(2,128)(2,1)S(1)} %copy.439), channel_id=1, source_target_pairs={{1,0},{2,1},{3,2},{0,3},{5,4},{6,5},{7,6},{4,7},{9,8},{10,9},{11,1... | collective-permute-start | bytes 3981320 | tf_op jit(solution)/shard_map/ppermute | solution.py:19
  1324.7 31.9 %collective-permute-start.47 = (bf16[2,6,36,1536]{3,0,2,1:T(2,128)(2,1)S(1)}, bf16[2,6,36,1536]{3,0,2,1:T(2,128)(2,1)S(1)}, u32[]{:S(2)}, u32[]{:S(2)}) collective-permute-start(bf16[2,6,36,1536]{3,0,2,1:T(2,128)(2,1)S(1)} %copy.439), channel_id=1, source_target_pairs={{0,1},{1,2},{2,3},{3,0},{4,5},{5,6},{6,7},{7,4},{8,9},{9,10},{10,1... | collective-permute-start | bytes 3981320 | tf_op jit(solution)/shard_map/ppermute | solution.py:17
  1450.3 29.4 %collective-permute-start.52 = (bf16[2,6,36,1536]{3,0,2,1:T(2,128)(2,1)S(1)}, bf16[2,6,36,1536]{3,0,2,1:T(2,128)(2,1)S(1)}, u32[]{:S(2)}, u32[]{:S(2)}) collective-permute-start(bf16[2,6,36,1536]{3,0,2,1:T(2,128)(2,1)S(1)} %copy.453), channel_id=1, source_target_pairs={{1,0},{2,1},{3,2},{0,3},{5,4},{6,5},{7,6},{4,7},{9,8},{10,9},{11,1... | collective-permute-start | bytes 3981320 | tf_op jit(solution)/shard_map/ppermute | solution.py:19
  1451.5 30.2 %collective-permute-start.51 = (bf16[2,6,36,1536]{3,0,2,1:T(2,128)(2,1)S(1)}, bf16[2,6,36,1536]{3,0,2,1:T(2,128)(2,1)S(1)}, u32[]{:S(2)}, u32[]{:S(2)}) collective-permute-start(bf16[2,6,36,1536]{3,0,2,1:T(2,128)(2,1)S(1)} %copy.453), channel_id=1, source_target_pairs={{0,1},{1,2},{2,3},{3,0},{4,5},{5,6},{6,7},{7,4},{8,9},{9,10},{10,1... | collective-permute-start | bytes 3981320 | tf_op jit(solution)/shard_map/ppermute | solution.py:17
  1575.7 30.9 %collective-permute-start.57 = (bf16[2,6,36,1536]{3,0,2,1:T(2,128)(2,1)}, bf16[2,6,36,1536]{3,0,2,1:T(2,128)(2,1)}, u32[]{:S(2)}, u32[]{:S(2)}) collective-permute-start(bf16[2,6,36,1536]{3,0,2,1:T(2,128)(2,1)} %copy.467), channel_id=1, source_target_pairs={{1,0},{2,1},{3,2},{0,3},{5,4},{6,5},{7,6},{4,7},{9,8},{10,9},{11,1... | collective-permute-start | bytes 3981320 | tf_op jit(solution)/shard_map/ppermute | solution.py:19
  1576.2 31.9 %collective-permute-start.56 = (bf16[2,6,36,1536]{3,0,2,1:T(2,128)(2,1)}, bf16[2,6,36,1536]{3,0,2,1:T(2,128)(2,1)}, u32[]{:S(2)}, u32[]{:S(2)}) collective-permute-start(bf16[2,6,36,1536]{3,0,2,1:T(2,128)(2,1)} %copy.467), channel_id=1, source_target_pairs={{0,1},{1,2},{2,3},{3,0},{4,5},{5,6},{6,7},{7,4},{8,9},{9,10},{10,1... | collective-permute-start | bytes 3981320 | tf_op jit(solution)/shard_map/ppermute | solution.py:17
  1696.1 28.8 %collective-permute-start.61 = (bf16[2,6,36,1536]{3,0,2,1:T(2,128)(2,1)S(1)}, bf16[2,6,36,1536]{3,0,2,1:T(2,128)(2,1)S(1)}, u32[]{:S(2)}, u32[]{:S(2)}) collective-permute-start(bf16[2,6,36,1536]{3,0,2,1:T(2,128)(2,1)S(1)} %copy.481), channel_id=1, source_target_pairs={{1,0},{2,1},{3,2},{0,3},{5,4},{6,5},{7,6},{4,7},{9,8},{10,9},{11,1... | collective-permute-start | bytes 3981320 | tf_op jit(solution)/shard_map/ppermute | solution.py:19
  1697.9 29.7 %collective-permute-start.60 = (bf16[2,6,36,1536]{3,0,2,1:T(2,128)(2,1)S(1)}, bf16[2,6,36,1536]{3,0,2,1:T(2,128)(2,1)S(1)}, u32[]{:S(2)}, u32[]{:S(2)}) collective-permute-start(bf16[2,6,36,1536]{3,0,2,1:T(2,128)(2,1)S(1)} %copy.481), channel_id=1, source_target_pairs={{0,1},{1,2},{2,3},{3,0},{4,5},{5,6},{6,7},{7,4},{8,9},{9,10},{10,1... | collective-permute-start | bytes 3981320 | tf_op jit(solution)/shard_map/ppermute | solution.py:17
  (125 other events, 1105.4 us)
where the time goes:
time: 1800 us; the launch traced here: 1790 us
  local copies, waits for them, and re-layouts  732 us (41%)
  waiting for transfers between devices  504 us (28%)
  other arithmetic  266 us (15%)
  matrix products  155 us (9%)
  starting transfers between devices  123 us (7%)
    ppermute x28, waiting for transfers between devices, extended(): lax.ppermute(head, axis, [((i + 1) % count, i) for i in range(count)])  385 us
    unnamed x232, local copies, waits for them, and re-layouts  163 us
    reshape x14, local copies, waits for them, and re-layouts, shards(): layer_packed.reshape(levels, ext_lat // W_LAT, W_LAT, ext_lon // W_LON, W...  130 us
    ppermute x28, waiting for transfers between devices, extended(): lax.ppermute(tail, axis, [(i, (i + 1) % count) for i in range(count)])  112 us
    ppermute x28, starting transfers between devices, extended(): lax.ppermute(head, axis, [((i + 1) % count, i) for i in range(count)])  95.3 us
    dot_general x14, matrix products, shards(): down = jnp.dot(hidden, w_down[inner], preferred_element_type=jnp.float32)  67.3 us
    dynamic_slice x14, local copies, waits for them, and re-layouts, shards(): layer_packed = jnp.roll(layer_packed, (-a_lat, -a_lon), axis=(1, 2))  59.3 us
    concatenate x28, other arithmetic, shards(): layer_packed = jnp.roll(layer_packed, (-a_lat, -a_lon), axis=(1, 2))  57.3 us
  transfers between devices with their start and end apart: 62, of which 47 were waited for; matrix products, arithmetic and copies ran while one was open for 1% of the time, Pallas kernels for 0%

commit v1 on v0

v1 whole, which is shorter than its diff:
```python
import functools

import jax
import jax.numpy as jnp
import numpy as np
from jax import lax
from jax.experimental import pallas as pl
from jax.experimental.pallas import tpu as pltpu
from jax.sharding import PartitionSpec as P

MESH = pl.DeviceIdType.MESH
HEADS = 8
GROUPS = 4
BLOCK = 36
HALF = GROUPS * BLOCK
CELLS = 2 * HALF
EDGE = 48
WIDE = CELLS + HALF + 3 * EDGE
PART = HALF // 2
SLOTS = 4
LOG2E = 1.4426950408889634
BIG = 1e30


def moves():
    table = np.zeros((CELLS, 128), np.float32)
    row = np.arange(CELLS)
    half, group, cell = row // HALF, row % HALF // BLOCK, row % BLOCK
    for lat in range(2):
        for lon in range(2):
            which = lat * 2 + lon
            for r in range(CELLS):
                h, g, t = half[r], group[r], cell[r]
                south, source = (h == 1, 1 - h) if lat else (False, h)
                east, column = (g == 3, (g + 1) % 4) if lon else (False, g)
                if south and east:
                    at = CELLS + HALF + 2 * EDGE + t
                elif south:
                    at = CELLS + column * BLOCK + t
                elif east:
                    at = CELLS + HALF + source * EDGE + t
                else:
                    at = source * HALF + column * BLOCK + t
                table[r, which] = at
                north, source = (h == 0, 1 - h) if lat else (False, h)
                west, column = (g == 0, (g + 3) % 4) if lon else (False, g)
                last = EDGE - BLOCK + t
                if north and west:
                    at = CELLS + HALF + 2 * EDGE + last
                elif north:
                    at = CELLS + column * BLOCK + t
                elif west:
                    at = CELLS + HALF + source * EDGE + last
                else:
                    at = source * HALF + column * BLOCK + t
                table[r, 4 + which] = at
    return table


def normed(values, gain):
    mean = jnp.mean(values, axis=-1, keepdims=True)
    centred = values - mean
    var = jnp.mean(centred * centred, axis=-1, keepdims=True)
    return centred * lax.rsqrt(var + 1e-05) * gain


def gelu(u):
    inner = u * (0.7978845608028654 + 0.035677408136300125 * (u * u))
    half = 0.5 * u
    return half + half * jnp.tanh(inner)


def dot(a, b):
    return jnp.dot(a, b, preferred_element_type=jnp.float32)


def kernel(
    lon_n, lat_n, depth_ref, latents, params, table, w_qkv, w_out, w_up, w_down, sections,
    wq, wo, wu, wd, par, fwd, bwd, x, src, ret, hid, stage, hand_out, hand_in, cross, ones,
    w_recv, w_send, p_recv, p_send, f_recv, f_send, b_recv, b_send, in_sem, h_recv, h_send,
    o_recv, o_send,
):
    seg = lax.axis_index("segment")
    lon = lax.axis_index("lon")
    lat = lax.axis_index("lat")
    chip = seg // 2
    core = lax.rem(seg, 2)
    mate_core = 1 - core
    north, south = lax.rem(lat + lat_n - 1, lat_n), lax.rem(lat + 1, lat_n)
    west, east = lax.rem(lon + lon_n - 1, lon_n), lax.rem(lon + 1, lon_n)

    def device(s, o, a):
        return {"segment": s, "lon": o, "lat": a}

    to_n, to_s = device(seg, lon, north), device(seg, lon, south)
    to_w, to_e = device(seg, west, lat), device(seg, east, lat)
    to_nw, to_se = device(seg, west, north), device(seg, east, south)
    mate = device(chip * 2 + mate_core, lon, lat)
    other = device(lax.rem(seg + 2, 4), lon, lat)

    weights = ((w_qkv, wq), (w_out, wo), (w_up, wu), (w_down, wd))

    def own_weights(i, k):
        slot = core * 2 + i
        held, kept = weights[k]
        return pltpu.make_async_copy(held.at[i], kept.at[slot], w_recv.at[slot, k])

    def lent_weights(i, k):
        slot = core * 2 + i
        held, kept = weights[k]
        return pltpu.make_async_remote_copy(
            src_ref=held.at[i], dst_ref=kept.at[slot], send_sem=w_send.at[i, k],
            recv_sem=w_recv.at[slot, k], device_id=mate, device_id_type=MESH,
        )

    def weights_here(l, k):
        held, kept = weights[k]
        pltpu.make_async_copy(held.at[0], kept.at[l], w_recv.at[l, k]).wait()

    def own_params():
        return pltpu.make_async_copy(params, par.at[pl.ds(core * 2, 2)], p_recv.at[core])

    def lent_params():
        return pltpu.make_async_remote_copy(
            src_ref=params, dst_ref=par.at[pl.ds(core * 2, 2)], send_sem=p_send.at[0],
            recv_sem=p_recv.at[core], device_id=mate, device_id_type=MESH,
        )

    def edges(b, buf, pieces, send, recv):
        return [
            pltpu.make_async_remote_copy(
                src_ref=buf.at[b, pl.ds(start, size)], dst_ref=buf.at[b, pl.ds(at, size)],
                send_sem=send.at[b, i], recv_sem=recv.at[b, i], device_id=to,
                device_id_type=MESH,
            )
            for i, (start, size, at, to) in enumerate(pieces)
        ]

    at_edge = CELLS + HALF

    def forth(b):
        return edges(
            b, src,
            (
                (0, HALF, CELLS, to_n),
                (0, EDGE, at_edge, to_w),
                (HALF, EDGE, at_edge + EDGE, to_w),
                (0, EDGE, at_edge + 2 * EDGE, to_nw),
            ),
            f_send, f_recv,
        )

    def back(b):
        return edges(
            b, ret,
            (
                (HALF, HALF, CELLS, to_s),
                (HALF - EDGE, EDGE, at_edge, to_e),
                (CELLS - EDGE, EDGE, at_edge + EDGE, to_e),
                (CELLS - EDGE, EDGE, at_edge + 2 * EDGE, to_se),
            ),
            b_send, b_recv,
        )

    def load_input(b):
        return pltpu.make_async_copy(
            latents.at[core + 2 * b], src.at[b, pl.ds(0, CELLS)], in_sem.at[b]
        )

    def hand_on(b):
        return pltpu.make_async_remote_copy(
            src_ref=hand_out.at[b], dst_ref=hand_in.at[b], send_sem=h_send.at[b],
            recv_sem=h_recv.at[b], device_id=other, device_id_type=MESH,
        )

    def keep_output(b, s):
        return pltpu.make_async_copy(
            stage.at[b, s], sections.at[core + 2 * b], o_recv.at[b, 0]
        )

    def give_output(b, s):
        return pltpu.make_async_remote_copy(
            src_ref=stage.at[b, s], dst_ref=sections.at[core + 2 * b], send_sem=o_send.at[b],
            recv_sem=o_recv.at[b, 1], device_id=mate, device_id_type=MESH,
        )

    barrier = pltpu.get_barrier_semaphore()
    for k in range(4):
        own_weights(0, k).start()
    own_params().start()

    @pl.when(chip == 0)
    def _():
        for b in range(2):
            load_input(b).start()

    for to in (to_n, to_s, to_w, to_e, to_nw, to_se, mate, other):
        pl.semaphore_signal(barrier, inc=1, device_id=to, device_id_type=MESH)
    pl.semaphore_wait(barrier, 8)

    lent_params().start()
    for i in range(2):
        for k in range(4):
            lent_weights(i, k).start()
            if i == 1:
                own_weights(i, k).start()

    @pl.when(chip == 0)
    def _():
        for b in range(2):
            load_input(b).wait()
            x[b] = src[b, 0:CELLS].astype(jnp.float32)
            for copy in forth(b):
                copy.start()

    @pl.when(chip == 1)
    def _():
        for b in range(2):
            hand_on(b).wait_recv()
            entry = hand_in[b]
            src[b, 0:CELLS] = entry
            x[b] = entry.astype(jnp.float32)
            for copy in forth(b):
                copy.start()

    own_params().wait()
    pltpu.make_async_copy(params, par.at[pl.ds(mate_core * 2, 2)], p_recv.at[mate_core]).wait()

    rows = lax.broadcasted_iota(jnp.int32, (HALF, HALF), 0)
    cols = lax.broadcasted_iota(jnp.int32, (HALF, HALF), 1)
    split = (rows < PART) != (cols < PART)
    is_last = jnp.where(lat == lat_n - 1, 1.0, 0.0)
    cross[...] = jnp.where(split, -BIG, 0.0) * is_last
    r256 = lax.broadcasted_iota(jnp.int32, (256, 256), 0)
    c256 = lax.broadcasted_iota(jnp.int32, (256, 256), 1)
    ones[...] = jnp.where(r256 // 64 == c256 // 64, 1.0, 0.0).astype(jnp.bfloat16)

    place = lax.broadcasted_iota(jnp.int32, (CELLS, WIDE), 1).astype(jnp.float32)

    def choose(l, carry):
        f_lat = par[l, 2:3, 0:1]
        f_lon = par[l, 3:4, 0:1]
        picks = (
            (1.0 - f_lat) * (1.0 - f_lon), (1.0 - f_lat) * f_lon,
            f_lat * (1.0 - f_lon), f_lat * f_lon,
        )
        for first, kept in ((0, fwd), (4, bwd)):
            at = sum(table[:, first + i : first + i + 1] * picks[i] for i in range(4))
            kept[l] = jnp.where(place == at, 1.0, 0.0).astype(jnp.bfloat16)
        return carry

    lax.fori_loop(0, SLOTS, choose, 0)

    lane = lax.broadcasted_iota(jnp.int32, (1, 256), 1)
    masks = [jnp.where(lane // 64 == h, 1.0, 0.0).astype(jnp.bfloat16) for h in range(4)]

    def unit(block):
        square = block * block
        high = square.astype(jnp.bfloat16)
        low = (square - high.astype(jnp.float32)).astype(jnp.bfloat16)
        total = dot(high, ones[...]) + dot(low, ones[...])
        return block * lax.rsqrt(total + 1e-06)

    def window(values, w):
        a = w * PART
        return jnp.concatenate(
            [values[a : a + PART], values[HALF + a : HALF + a + PART]], axis=0
        ).astype(jnp.bfloat16)

    def attend(b, l):
        for copy in forth(b):
            copy.wait()
        cells = dot(fwd[l], src[b]).astype(jnp.bfloat16)
        bias = par[l, 2:3, 0:HALF] * cross[...]
        for g in range(2):
            lanes = [slice(p * 512 + g * 256, p * 512 + g * 256 + 256) for p in range(3)]
            q = unit(dot(cells, wq[l, :, lanes[0]]))
            k = unit(dot(cells, wq[l, :, lanes[1]]))
            v = dot(cells, wq[l, :, lanes[2]])
            outs = []
            for w in range(2):
                qw, kw, vw = window(q, w), window(k, w), window(v, w)
                total = jnp.zeros((HALF, 256), jnp.float32)
                for h in range(4):
                    scale = par[l, 4 + g * 4 + h : 5 + g * 4 + h, 0:HALF]
                    score = lax.dot_general(
                        qw, kw * masks[h], (((1,), (1,)), ((), ())),
                        preferred_element_type=jnp.float32,
                    )
                    score = score * scale + bias
                    top = jnp.max(score, axis=-1, keepdims=True)
                    expo = jnp.exp2(score - top)
                    share = 1.0 / jnp.sum(expo, axis=-1, keepdims=True)
                    weight = (expo * share).astype(jnp.bfloat16)
                    total = total + dot(weight, vw * masks[h])
                outs.append(total)
            for h in range(2):
                part = slice(h * PART, h * PART + PART)
                ret[b, h * HALF : h * HALF + HALF, g * 256 : g * 256 + 256] = jnp.concatenate(
                    [outs[0][part], outs[1][part]], axis=0
                ).astype(jnp.bfloat16)
        for copy in back(b):
            copy.start()

    def feed(b, l):
        for copy in back(b):
            copy.wait()
        mixed = dot(bwd[l], ret[b]).astype(jnp.bfloat16)
        state = x[b]
        first = state + normed(dot(mixed, wo[l]), par[l, 0:1])
        firstb = first.astype(jnp.bfloat16)
        for c in range(4):
            part = slice(c * 512, c * 512 + 512)
            hid[:, part] = gelu(dot(firstb, wu[l, :, part])).astype(jnp.bfloat16)
        second = first + normed(dot(hid[...], wd[l]), par[l, 1:2])
        s = l // 2
        applied = lax.rem(l, 2) < depth_ref[chip * 2 + s]
        fresh = jnp.where(applied, second, state)
        x[b] = fresh
        freshb = fresh.astype(jnp.bfloat16)

        @pl.when(l < SLOTS - 1)
        def _():
            src[b, 0:CELLS] = freshb
            for copy in forth(b):
                copy.start()

        @pl.when(lax.rem(l, 2) == 1)
        def _():
            stage[b, s] = fresh

            @pl.when(s == core)
            def _():
                keep_output(b, s).start()

            @pl.when(s != core)
            def _():
                give_output(b, s).start()

        @pl.when((l == SLOTS - 1) & (chip == 0))
        def _():
            hand_out[b] = freshb
            hand_on(b).start()

    def layer(l, carry):
        weights_here(l, 0)

        def one(b, c):
            attend(b, l)
            return c

        lax.fori_loop(0, 2, one, 0)
        for k in range(1, 4):
            weights_here(l, k)

        def two(b, c):
            feed(b, l)
            return c

        lax.fori_loop(0, 2, two, 0)
        return carry

    lax.fori_loop(0, SLOTS, layer, 0)

    for i in range(2):
        for k in range(4):
            lent_weights(i, k).wait_send()
    lent_params().wait_send()

    @pl.when(chip == 0)
    def _():
        for b in range(2):
            hand_on(b).wait_send()

    for b in range(2):
        keep_output(b, core).wait()
        give_output(b, mate_core).wait()


def shards(latents, segment_depth, shift_flags, w_qkv, w_out, w_up, w_down, gains, logit_scale,
           lon_n, lat_n):
    micro, levels, clat, clon, width = latents.shape
    cells = latents.reshape(micro, levels, 2, 3, GROUPS, 6, width)
    cells = cells.transpose(0, 2, 4, 1, 3, 5, 6).reshape(micro, CELLS, width)
    small = jnp.concatenate(
        [shift_flags.astype(jnp.float32), logit_scale * LOG2E, jnp.zeros((2, 4), jnp.float32)],
        axis=1,
    )
    params = jnp.concatenate(
        [gains, jnp.broadcast_to(small[:, :, None], (2, 14, width))], axis=1
    )
    table = jnp.asarray(moves())
    hbm = pl.BlockSpec(memory_space=pl.ANY)
    bf16, f32 = jnp.bfloat16, jnp.float32
    dma = pltpu.SemaphoreType.DMA
    out = pl.pallas_call(
        functools.partial(kernel, lon_n, lat_n),
        out_shape=jax.ShapeDtypeStruct((micro, CELLS, width), f32),
        in_specs=[
            pl.BlockSpec(memory_space=pltpu.SMEM), hbm, hbm,
            pl.BlockSpec(memory_space=pltpu.VMEM), hbm, hbm, hbm, hbm,
        ],
        out_specs=hbm,
        scratch_shapes=[
            pltpu.VMEM((SLOTS, width, 3 * width), bf16),
            pltpu.VMEM((SLOTS, width, width), bf16),
            pltpu.VMEM((SLOTS, width, 4 * width), bf16),
            pltpu.VMEM((SLOTS, 4 * width, width), bf16),
            pltpu.VMEM((SLOTS, 16, width), f32),
            pltpu.VMEM((SLOTS, CELLS, WIDE), bf16),
            pltpu.VMEM((SLOTS, CELLS, WIDE), bf16),
            pltpu.VMEM((2, CELLS, width), f32),
            pltpu.VMEM((2, WIDE, width), bf16),
            pltpu.VMEM((2, WIDE, width), bf16),
            pltpu.VMEM((CELLS, 4 * width), bf16),
            pltpu.VMEM((2, 2, CELLS, width), f32),
            pltpu.VMEM((2, CELLS, width), bf16),
            pltpu.VMEM((2, CELLS, width), bf16),
            pltpu.VMEM((HALF, HALF), f32),
            pltpu.VMEM((256, 256), bf16),
            dma((SLOTS, 4)), dma((2, 4)), dma((2,)), dma((1,)),
            dma((2, 4)), dma((2, 4)), dma((2, 4)), dma((2, 4)),
            dma((2,)), dma((2,)), dma((2,)), dma((2, 2)), dma((2,)),
        ],
        compiler_params=pltpu.CompilerParams(
            collective_id=0, has_side_effects=True, vmem_limit_bytes=60 * 1024 * 1024
        ),
        cost_estimate=pl.CostEstimate(
            flops=16 * 2 * 10**9, bytes_accessed=20 * 10**6, transcendentals=10**7
        ),
    )(segment_depth, cells, params, table, w_qkv, w_out, w_up, w_down)
    out = out.reshape(micro, 2, GROUPS, levels, 3, 6, width).transpose(0, 3, 1, 4, 2, 5, 6)
    return out.reshape(1, micro, levels, clat, clon, width)


def solution(mesh):
    placed = (
        P(None, None, "lat", "lon", None),
        P(),
        P("segment", None),
        P("segment", None, None),
        P("segment", None, None),
        P("segment", None, None),
        P("segment", None, None),
        P("segment", None, None),
        P("segment", None),
    )
    return jax.shard_map(
        functools.partial(shards, lon_n=mesh.shape["lon"], lat_n=mesh.shape["lat"]),
        mesh=mesh,
        in_specs=placed,
        out_specs=P("segment", None, None, "lat", "lon", None),
        check_vma=False,
    )
```

time: 1800 us -> 217 us (0.12)
  the two profiles are of different devices: /device:TPU:0 before, /device:TPU:33 now
where the time goes in v1:
time: 217 us; the launch traced here: 216 us
  Pallas kernels  202 us (93%)
  local copies, waits for them, and re-layouts  11.6 us (5%)
  other arithmetic  2.76 us (1%)
    pallas_call x1, Pallas kernels, shards(): pl.pallas_call(functools.partial(kernel, lon_n, lat_n), out_shape=jax.Sha...  202 us

profile of v1, /device:TPU:33, one launch (start us, length us, event | category | flops | bytes accessed | tf_op | source)
XLA Modules:
  0.0 216.3 jit_solution(17204261726523635793)
XLA Ops:
  0.0 0.1 pad.4.clone
  0.1 0.7 convert_element_type.3
  0.8 0.7 broadcast_multiply_fusion
  1.4 0.1 maximum_maximum_fusion
  1.5 0.1 broadcast_in_dim.2
  1.6 1.3 pad_maximum_fusion.params
  2.9 2.5 %copy.13 = bf16[4,2,6,24,512]{4,1,3,2,0:T(2,128)(2,1)S(1)} copy(bf16[4,2,6,24,512]{4,3,2,1,0:T(8,128)(2,1)} %param.10) | data formatting | bytes 2359296 | tf_op args[0]
  5.4 0.9 copy.14
  6.3 1.2 copy.15.latents
  7.6 201.9 %shard_map.100 = f32[4,288,512]{2,1,0:T(8,128)} custom-call(s32[4]{0:T(128)} %depth_ref.1, bf16[4,288,512]{2,1,0:T(8,128)(2,1)} %copy.15.latents, f32[2,16,512]{2,1,0:T(8,128)} %pad_maximum_fusion.params, f32[288,128]{1,0:T(8,128)} %constant.6.clone.table, bf16[2,512,1536]{2,1,0:T(8,128)(2,1)} %w_qkv.1, bf16[2,512,512]{2,1,0:T(8,128)(2,1)} %w_out.1, ...), custom_call_target="tpu_custom_call" | custom-call | flops 32000000000 | bytes 20000000 | tf_op jit(solution)/shard_map/pallas_call | solution.py:396
  209.4 3.2 %copy.16 = f32[4,288,512]{2,0,1:T(4,128)S(1)} copy(f32[4,288,512]{2,1,0:T(8,128)} %shard_map.100) | data formatting | bytes 4718592 | tf_op jit(solution)/shard_map/pallas_call | solution.py:396
  212.6 1.8 copy.17
  214.5 1.8 copy.18
  (1 shorter events, 0.0 us)

commit v2 on v1

v2 whole, which is shorter than its diff:
```python
import functools

import jax
import jax.numpy as jnp
import numpy as np
from jax import lax
from jax.experimental import pallas as pl
from jax.experimental.pallas import tpu as pltpu
from jax.sharding import PartitionSpec as P

MESH = pl.DeviceIdType.MESH
HALF = 144
CELLS = 2 * HALF
PART = HALF // 2
REACH = 80
EDGE = 48
AT_LAT = CELLS
AT_LON = AT_LAT + 2 * REACH
AT_BOTH = AT_LON + 2 * EDGE
WIDE = AT_BOTH + EDGE
SLOTS = 4
LOG2E = 1.4426950408889634
BIG = 1e30


def moves():
    table = np.zeros((CELLS, 128), np.float32)
    for core in range(2):
        far_half = 1 - core
        for lat in range(2):
            for lon in range(2):
                which = core * 8 + lat * 2 + lon
                for at in range(CELLS):
                    window, half, pair, cell = at // 144, at % 144 // 72, at % 72 // 36, at % 36
                    level, row, column = cell // 18, cell % 18 // 6, cell % 6
                    column += (2 * window + pair) * 6 + lon * (6 - 12 * core)
                    across = column >= 24 or column < 0
                    edge_column = column - 24 if core == 0 else column + 24 - 16
                    along = lat == 1 and half == far_half
                    source = 1 - half if lat else half
                    edge = (level * 3 + row) * 8 + edge_column
                    if along and across:
                        take = AT_BOTH + edge
                    elif along:
                        take = AT_LAT + level * REACH + core * 8 + row * 24 + column
                    elif across:
                        take = AT_LON + source * EDGE + edge
                    else:
                        take = level * 144 + (source * 3 + row) * 24 + column
                    table[at, which] = take

                    level, row, column = at // 144, at % 144 // 24, at % 24
                    half, row = row // 3, row % 3
                    along = lat == 1 and half == core
                    source = 1 - half if lat else half
                    column -= lon * (6 - 12 * core)
                    across = column >= 24 or column < 0
                    column %= 24
                    window, pair = column // 12, column % 12 // 6
                    inside = source * 72 + pair * 36 + level * 18 + row * 6 + column % 6
                    if along and across:
                        take = AT_BOTH + inside - (0 if core else 96)
                    elif along:
                        take = AT_LAT + window * REACH + inside - (0 if core else 64)
                    elif across:
                        take = AT_LON + source * EDGE + inside - source * 64 - (0 if core else 32)
                    else:
                        take = window * 144 + inside
                    table[at, which + 4] = take
    return table


def normed(values, gain):
    mean = jnp.mean(values, axis=-1, keepdims=True)
    centred = values - mean
    var = jnp.mean(centred * centred, axis=-1, keepdims=True)
    return centred * lax.rsqrt(var + 1e-05) * gain


def gelu(u):
    inner = u * (0.7978845608028654 + 0.035677408136300125 * (u * u))
    half = 0.5 * u
    return half + half * jnp.tanh(inner)


def dot(a, b):
    return jnp.dot(a, b, preferred_element_type=jnp.float32)


def kernel(
    lon_n, lat_n, depth_ref, latents, small_in, gains_in, table, w_qkv, w_out, w_up, w_down, sections,
    wq, wo, wu, wd, small, gains, fwd, bwd, x, src, packed, ret, hid, stage, hand_out, hand_in, cross, ones,
    w_recv, w_send, p_recv, p_send, f_recv, f_send, b_recv, b_send, in_sem, h_recv, h_send,
    o_recv, o_send,
):
    seg = lax.axis_index("segment")
    lon = lax.axis_index("lon")
    lat = lax.axis_index("lat")
    chip = seg // 2
    core = lax.rem(seg, 2)
    mate_core = 1 - core
    north, south = lax.rem(lat + lat_n - 1, lat_n), lax.rem(lat + 1, lat_n)
    west, east = lax.rem(lon + lon_n - 1, lon_n), lax.rem(lon + 1, lon_n)

    def device(s, o, a):
        return {"segment": s, "lon": o, "lat": a}

    out_lat, home_lat = north + core * (south - north), south + core * (north - south)
    out_lon, home_lon = west + core * (east - west), east + core * (west - east)
    to_n, to_s = device(seg, lon, out_lat), device(seg, lon, home_lat)
    to_w, to_e = device(seg, out_lon, lat), device(seg, home_lon, lat)
    to_nw, to_se = device(seg, out_lon, out_lat), device(seg, home_lon, home_lat)
    mate = device(chip * 2 + mate_core, lon, lat)
    other = device(lax.rem(seg + 2, 4), lon, lat)

    weights = ((w_qkv, wq), (w_out, wo), (w_up, wu), (w_down, wd))

    def own_weights(i, k):
        slot = core * 2 + i
        held, kept = weights[k]
        return pltpu.make_async_copy(held.at[i], kept.at[slot], w_recv.at[slot, k])

    def lent_weights(i, k):
        slot = core * 2 + i
        held, kept = weights[k]
        return pltpu.make_async_remote_copy(
            src_ref=held.at[i], dst_ref=kept.at[slot], send_sem=w_send.at[i, k],
            recv_sem=w_recv.at[slot, k], device_id=mate, device_id_type=MESH,
        )

    def weights_here(l, k):
        held, kept = weights[k]
        pltpu.make_async_copy(held.at[0], kept.at[l], w_recv.at[l, k]).wait()

    tiny = ((small_in, small), (gains_in, gains))

    def own_params(k):
        held, kept = tiny[k]
        return pltpu.make_async_copy(held, kept.at[pl.ds(core * 2, 2)], p_recv.at[core, k])

    def lent_params(k):
        held, kept = tiny[k]
        return pltpu.make_async_remote_copy(
            src_ref=held, dst_ref=kept.at[pl.ds(core * 2, 2)], send_sem=p_send.at[k],
            recv_sem=p_recv.at[core, k], device_id=mate, device_id_type=MESH,
        )

    def edges(pieces, send, recv):
        return [
            pltpu.make_async_remote_copy(
                src_ref=source, dst_ref=target, send_sem=send.at[i], recv_sem=recv.at[i],
                device_id=to, device_id_type=MESH,
            )
            for i, (source, target, to) in enumerate(pieces)
        ]

    def rows_from(start, size):
        return pl.ds(pl.multiple_of(start, 16), size)

    def forth(b):
        return edges(
            (
                (src.at[b, rows_from(64 * core, REACH)], src.at[b, pl.ds(AT_LAT, REACH)], to_n),
                (
                    src.at[b, rows_from(HALF + 64 * core, REACH)],
                    src.at[b, pl.ds(AT_LAT + REACH, REACH)], to_n,
                ),
                (packed.at[b], src.at[b, pl.ds(AT_LON, 2 * EDGE)], to_w),
                (packed.at[b, rows_from(EDGE * core, EDGE)], src.at[b, pl.ds(AT_BOTH, EDGE)], to_nw),
            ),
            f_send.at[b], f_recv.at[b],
        )

    def back(b):
        return edges(
            (
                (ret.at[b, rows_from(64 - 64 * core, REACH)], ret.at[b, pl.ds(AT_LAT, REACH)], to_s),
                (
                    ret.at[b, rows_from(208 - 64 * core, REACH)],
                    ret.at[b, pl.ds(AT_LAT + REACH, REACH)], to_s,
                ),
                (ret.at[b, rows_from(176 - 176 * core, EDGE)], ret.at[b, pl.ds(AT_LON, EDGE)], to_e),
                (
                    ret.at[b, rows_from(240 - 176 * core, EDGE)],
                    ret.at[b, pl.ds(AT_LON + EDGE, EDGE)], to_e,
                ),
                (ret.at[b, rows_from(240 - 240 * core, EDGE)], ret.at[b, pl.ds(AT_BOTH, EDGE)], to_se),
            ),
            b_send.at[b], b_recv.at[b],
        )

    def edge_of(values, column):
        rows = [
            level * 144 + row * 24 + column
            for half in ((0, 1, 2), (3, 4, 5)) for level in (0, 1) for row in half
        ]
        return jnp.concatenate([values[r : r + 8] for r in rows], axis=0)

    def far_edge(values):
        return jnp.where(core == 0, edge_of(values, 0), edge_of(values, 16)).astype(jnp.bfloat16)

    def load_input(b):
        return pltpu.make_async_copy(
            latents.at[core + 2 * b], src.at[b, pl.ds(0, CELLS)], in_sem.at[b]
        )

    def hand_on(b):
        return pltpu.make_async_remote_copy(
            src_ref=hand_out.at[b], dst_ref=hand_in.at[b], send_sem=h_send.at[b],
            recv_sem=h_recv.at[b], device_id=other, device_id_type=MESH,
        )

    def keep_output(b, s):
        return pltpu.make_async_copy(
            stage.at[b, s], sections.at[core + 2 * b], o_recv.at[b, 0]
        )

    def give_output(b, s):
        return pltpu.make_async_remote_copy(
            src_ref=stage.at[b, s], dst_ref=sections.at[core + 2 * b], send_sem=o_send.at[b],
            recv_sem=o_recv.at[b, 1], device_id=mate, device_id_type=MESH,
        )

    barrier = pltpu.get_barrier_semaphore()
    for k in range(4):
        own_weights(0, k).start()
    for k in range(2):
        own_params(k).start()

    @pl.when(chip == 0)
    def _():
        for b in range(2):
            load_input(b).start()

    for to in (to_n, to_s, to_w, to_e, to_nw, to_se, mate, other):
        pl.semaphore_signal(barrier, inc=1, device_id=to, device_id_type=MESH)
    pl.semaphore_wait(barrier, 8)

    for k in range(2):
        lent_params(k).start()
    for i in range(2):
        for k in range(4):
            lent_weights(i, k).start()
            if i == 1:
                own_weights(i, k).start()

    @pl.when(chip == 0)
    def _():
        for b in range(2):
            load_input(b).wait()
            entry = src[b, 0:CELLS].astype(jnp.float32)
            x[b] = entry
            packed[b] = far_edge(entry)
            for copy in forth(b):
                copy.start()

    @pl.when(chip == 1)
    def _():
        for b in range(2):
            hand_on(b).wait_recv()
            src[b, 0:CELLS] = hand_in[b]
            entry = hand_in[b].astype(jnp.float32)
            x[b] = entry
            packed[b] = far_edge(entry)
            for copy in forth(b):
                copy.start()

    for k, (held, kept) in enumerate(tiny):
        own_params(k).wait()
        pltpu.make_async_copy(
            held, kept.at[pl.ds(mate_core * 2, 2)], p_recv.at[mate_core, k]
        ).wait()

    rows = lax.broadcasted_iota(jnp.int32, (HALF, HALF), 0)
    cols = lax.broadcasted_iota(jnp.int32, (HALF, HALF), 1)
    split = (rows < PART) != (cols < PART)
    is_last = jnp.where(lat == (lat_n - 1) * (1 - core), 1.0, 0.0)
    cross[...] = jnp.where(split, -BIG, 0.0) * is_last
    r256 = lax.broadcasted_iota(jnp.int32, (256, 256), 0)
    c256 = lax.broadcasted_iota(jnp.int32, (256, 256), 1)
    ones[...] = jnp.where(r256 // 64 == c256 // 64, 1.0, 0.0).astype(jnp.bfloat16)

    place = lax.broadcasted_iota(jnp.int32, (CELLS, WIDE), 1).astype(jnp.float32)

    def choose(l, carry):
        f_lat = small[l, 0:1, 0:1]
        f_lon = small[l, 0:1, 1:2]
        picks = (
            (1.0 - f_lat) * (1.0 - f_lon), (1.0 - f_lat) * f_lon,
            f_lat * (1.0 - f_lon), f_lat * f_lon,
        )
        for first, kept in ((0, fwd), (4, bwd)):
            at = sum(
                jnp.where(
                    core == 0, table[:, first + i : first + i + 1],
                    table[:, first + i + 8 : first + i + 9],
                ) * picks[i]
                for i in range(4)
            )
            kept[l] = jnp.where(place == at, 1.0, 0.0).astype(jnp.bfloat16)
        return carry

    lax.fori_loop(0, SLOTS, choose, 0)

    lane = lax.broadcasted_iota(jnp.int32, (1, 256), 1)
    masks = [jnp.where(lane // 64 == h, 1.0, 0.0).astype(jnp.bfloat16) for h in range(4)]
    first_of_pair = lax.broadcasted_iota(jnp.int32, (HALF, 128), 1) < 64

    def unit(block):
        total = dot((block * block).astype(jnp.bfloat16), ones[...])
        return (block * lax.rsqrt(total + 1e-06)).astype(jnp.bfloat16)

    def attend(b, l):
        for copy in forth(b):
            copy.wait()
        cells = dot(fwd[l], src[b]).astype(jnp.bfloat16)
        bias = small[l, 0:1, 0:1] * cross[...]
        for g in range(2):
            lanes = [slice(p * 512 + g * 256, p * 512 + g * 256 + 256) for p in range(3)]
            q = unit(dot(cells, wq[l, :, lanes[0]]))
            k = unit(dot(cells, wq[l, :, lanes[1]]))
            v = dot(cells, wq[l, :, lanes[2]]).astype(jnp.bfloat16)
            for w in range(2):
                part = slice(w * HALF, w * HALF + HALF)
                heads = jnp.concatenate([q[part] * masks[h] for h in range(4)], axis=0)
                scores = lax.dot_general(
                    heads, k[part], (((1,), (1,)), ((), ())), preferred_element_type=jnp.float32
                )
                expos, shares = [], []
                for h in range(4):
                    scale = small[l, 0:1, 2 + g * 4 + h : 3 + g * 4 + h]
                    score = scores[h * HALF : h * HALF + HALF] * scale + bias
                    expo = jnp.exp2(score - jnp.max(score, axis=-1, keepdims=True))
                    shares.append(1.0 / jnp.sum(expo, axis=-1, keepdims=True))
                    expos.append(expo.astype(jnp.bfloat16))
                mixed = dot(jnp.concatenate(expos, axis=0), v[part])
                for p in range(2):
                    at = slice(p * 128, p * 128 + 128)
                    one = mixed[2 * p * HALF : (2 * p + 1) * HALF, at] * shares[2 * p]
                    two = mixed[(2 * p + 1) * HALF : (2 * p + 2) * HALF, at] * shares[2 * p + 1]
                    ret[b, part, g * 256 + p * 128 : g * 256 + p * 128 + 128] = jnp.where(
                        first_of_pair, one, two
                    ).astype(jnp.bfloat16)
        for copy in back(b):
            copy.start()

    def feed(b, l):
        for copy in back(b):
            copy.wait()
        mixed = dot(bwd[l], ret[b]).astype(jnp.bfloat16)
        state = x[b]
        first = state + normed(dot(mixed, wo[l]), gains[l, 0:1])
        firstb = first.astype(jnp.bfloat16)
        for c in range(4):
            part = slice(c * 512, c * 512 + 512)
            hid[:, part] = gelu(dot(firstb, wu[l, :, part])).astype(jnp.bfloat16)
        second = first + normed(dot(hid[...], wd[l]), gains[l, 1:2])
        s = l // 2
        applied = lax.rem(l, 2) < depth_ref[chip * 2 + s]
        fresh = jnp.where(applied, second, state)
        x[b] = fresh
        freshb = fresh.astype(jnp.bfloat16)

        @pl.when(l < SLOTS - 1)
        def _():
            src[b, 0:CELLS] = freshb
            packed[b] = far_edge(fresh)
            for copy in forth(b):
                copy.start()

        @pl.when(lax.rem(l, 2) == 1)
        def _():
            stage[b, s] = fresh

            @pl.when(s == core)
            def _():
                keep_output(b, s).start()

            @pl.when(s != core)
            def _():
                give_output(b, s).start()

        @pl.when((l == SLOTS - 1) & (chip == 0))
        def _():
            hand_out[b] = freshb
            hand_on(b).start()

    def layer(l, carry):
        weights_here(l, 0)

        def one(b, c):
            attend(b, l)
            return c

        lax.fori_loop(0, 2, one, 0)
        for k in range(1, 4):
            weights_here(l, k)

        def two(b, c):
            feed(b, l)
            return c

        lax.fori_loop(0, 2, two, 0)
        return carry

    lax.fori_loop(0, SLOTS, layer, 0)

    for i in range(2):
        for k in range(4):
            lent_weights(i, k).wait_send()
    for k in range(2):
        lent_params(k).wait_send()

    @pl.when(chip == 0)
    def _():
        for b in range(2):
            hand_on(b).wait_send()

    for b in range(2):
        keep_output(b, core).wait()
        give_output(b, mate_core).wait()


def shards(latents, segment_depth, shift_flags, w_qkv, w_out, w_up, w_down, gains, logit_scale,
           lon_n, lat_n):
    micro, levels, clat, clon, width = latents.shape
    cells = latents.reshape(micro, CELLS, width)
    small = jnp.concatenate(
        [shift_flags.astype(jnp.float32), logit_scale * LOG2E, jnp.zeros((2, 118), jnp.float32)],
        axis=1,
    ).reshape(2, 1, 128)
    table = jnp.asarray(moves())
    hbm = pl.BlockSpec(memory_space=pl.ANY)
    bf16, f32 = jnp.bfloat16, jnp.float32
    dma = pltpu.SemaphoreType.DMA
    out = pl.pallas_call(
        functools.partial(kernel, lon_n, lat_n),
        out_shape=jax.ShapeDtypeStruct((micro, CELLS, width), f32),
        in_specs=[
            pl.BlockSpec(memory_space=pltpu.SMEM), hbm, hbm, hbm,
            pl.BlockSpec(memory_space=pltpu.VMEM), hbm, hbm, hbm, hbm,
        ],
        out_specs=hbm,
        scratch_shapes=[
            pltpu.VMEM((SLOTS, width, 3 * width), bf16),
            pltpu.VMEM((SLOTS, width, width), bf16),
            pltpu.VMEM((SLOTS, width, 4 * width), bf16),
            pltpu.VMEM((SLOTS, 4 * width, width), bf16),
            pltpu.VMEM((SLOTS, 1, 128), f32),
            pltpu.VMEM((SLOTS, 2, width), f32),
            pltpu.VMEM((SLOTS, CELLS, WIDE), bf16),
            pltpu.VMEM((SLOTS, CELLS, WIDE), bf16),
            pltpu.VMEM((2, CELLS, width), f32),
            pltpu.VMEM((2, WIDE, width), bf16),
            pltpu.VMEM((2, 2 * EDGE, width), bf16),
            pltpu.VMEM((2, WIDE, width), bf16),
            pltpu.VMEM((CELLS, 4 * width), bf16),
            pltpu.VMEM((2, 2, CELLS, width), f32),
            pltpu.VMEM((2, CELLS, width), bf16),
            pltpu.VMEM((2, CELLS, width), bf16),
            pltpu.VMEM((HALF, HALF), f32),
            pltpu.VMEM((256, 256), bf16),
            dma((SLOTS, 4)), dma((2, 4)), dma((2, 2)), dma((2,)),
            dma((2, 4)), dma((2, 4)), dma((2, 5)), dma((2, 5)),
            dma((2,)), dma((2,)), dma((2,)), dma((2, 2)), dma((2,)),
        ],
        compiler_params=pltpu.CompilerParams(
            collective_id=0, has_side_effects=True, vmem_limit_bytes=60 * 1024 * 1024
        ),
        cost_estimate=pl.CostEstimate(
            flops=16 * 2 * 10**9, bytes_accessed=20 * 10**6, transcendentals=10**7
        ),
    )(segment_depth, cells, small, gains, table, w_qkv, w_out, w_up, w_down)
    return out.reshape(1, micro, levels, clat, clon, width)


def solution(mesh):
    placed = (
        P(None, None, "lat", "lon", None),
        P(),
        P("segment", None),
        P("segment", None, None),
        P("segment", None, None),
        P("segment", None, None),
        P("segment", None, None),
        P("segment", None, None),
        P("segment", None),
    )
    return jax.shard_map(
        functools.partial(shards, lon_n=mesh.shape["lon"], lat_n=mesh.shape["lat"]),
        mesh=mesh,
        in_specs=placed,
        out_specs=P("segment", None, None, "lat", "lon", None),
        check_vma=False,
    )
```

time: 217 us -> 205 us (0.945)
  local copies, waits for them, and re-layouts: 11.6 us -> 3.42 us
  Pallas kernels: 202 us -> 199 us
    pallas_call x1 -> x0, local copies, waits for them, and re-layouts: 3.18 us -> none  [shards(): pl.pallas_call(functools.partial(kernel, lon_n, lat_n), out_shape=jax.Sha...]
    reshape x2 -> x0, local copies, waits for them, and re-layouts: 3.07 us -> none  [the longest x1 1.84 us: shards(): return out.reshape(1, micro, levels, clat, clon, width)]
    transpose x2 -> x0, local copies, waits for them, and re-layouts: 2.74 us -> none  [the longest x1 1.82 us: shards(): out.reshape(micro, 2, GROUPS, levels, 3, 6, width)]
    pallas_call x1, Pallas kernels: 202 us -> 199 us  [shards(): pl.pallas_call(functools.partial(kernel, lon_n, lat_n), out_shape=jax.Sha...]
where the time goes in v2:
time: 205 us
  Pallas kernels  199 us (97%)
  local copies, waits for them, and re-layouts  3.42 us (2%)
    pallas_call x1, Pallas kernels, shards(): pl.pallas_call(functools.partial(kernel, lon_n, lat_n), out_shape=jax.Sha...  199 us

profile of v2, /device:TPU:33, one launch (start us, length us, event | category | flops | bytes accessed | tf_op | source)
XLA Modules:
  0.0 204.8 jit_solution(8668758319249186436)
XLA Ops:
  0.0 0.1 pad.2.clone
  0.1 0.7 convert_element_type.3
  0.8 0.7 broadcast_multiply_fusion
  1.4 0.6 maximum_maximum_fusion
  2.1 199.4 %shard_map.100 = f32[4,288,512]{2,1,0:T(8,128)} custom-call(s32[4]{0:T(128)} %depth_ref.1, bf16[4,288,512]{2,1,0:T(8,128)(2,1)} %bitcast.5, f32[2,1,128]{2,1,0:T(1,128)} %bitcast.4, f32[2,2,512]{2,1,0:T(2,128)} %gains_in.1, f32[288,128]{1,0:T(8,128)} %constant.6.clone.table, bf16[2,512,1536]{2,1,0:T(8,128)(2,1)} %w_qkv.1, bf16[2,512,512]{2,1,0:T(8,128)(2,1)} %w_out.1, ...), custom_call_target="tpu_custom_call" | custom-call | flops 32000000000 | bytes 20000000 | tf_op jit(solution)/shard_map/pallas_call | solution.py:436
  201.4 3.3 %copy.12 = f32[1,4,2,6,24,512]{5,4,3,2,1,0:T(8,128)} copy(f32[1,4,2,6,24,512]{5,4,3,2,1,0:T(8,128)} %bitcast.3) | data formatting | bytes 4718592
  (1 shorter events, 0.0 us)

commit v3 on v2

--- a/solution.py
+++ b/solution.py
@@ -89,7 +89,7 @@
 
 def kernel(
     lon_n, lat_n, depth_ref, latents, small_in, gains_in, table, w_qkv, w_out, w_up, w_down, sections,
-    wq, wo, wu, wd, small, gains, fwd, bwd, x, src, packed, ret, hid, stage, hand_out, hand_in, cross, ones,
+    wq, wo, wu, wd, small, gains, fwd, bwd, x, src, packed, ret, stage, hand_out, hand_in, cross, ones,
     w_recv, w_send, p_recv, p_send, f_recv, f_send, b_recv, b_send, in_sem, h_recv, h_send,
     o_recv, o_send,
 ):
@@ -315,6 +315,7 @@
             copy.wait()
         cells = dot(fwd[l], src[b]).astype(jnp.bfloat16)
         bias = small[l, 0:1, 0:1] * cross[...]
+        done = [[], []]
         for g in range(2):
             lanes = [slice(p * 512 + g * 256, p * 512 + g * 256 + 256) for p in range(3)]
             q = unit(dot(cells, wq[l, :, lanes[0]]))
@@ -338,9 +339,9 @@
                     at = slice(p * 128, p * 128 + 128)
                     one = mixed[2 * p * HALF : (2 * p + 1) * HALF, at] * shares[2 * p]
                     two = mixed[(2 * p + 1) * HALF : (2 * p + 2) * HALF, at] * shares[2 * p + 1]
-                    ret[b, part, g * 256 + p * 128 : g * 256 + p * 128 + 128] = jnp.where(
-                        first_of_pair, one, two
-                    ).astype(jnp.bfloat16)
+                    done[w].append(jnp.where(first_of_pair, one, two).astype(jnp.bfloat16))
+        for w in range(2):
+            ret[b, w * HALF : w * HALF + HALF] = jnp.concatenate(done[w], axis=1)
         for copy in back(b):
             copy.start()
 
@@ -351,10 +352,14 @@
         state = x[b]
         first = state + normed(dot(mixed, wo[l]), gains[l, 0:1])
         firstb = first.astype(jnp.bfloat16)
-        for c in range(4):
-            part = slice(c * 512, c * 512 + 512)
-            hid[:, part] = gelu(dot(firstb, wu[l, :, part])).astype(jnp.bfloat16)
-        second = first + normed(dot(hid[...], wd[l]), gains[l, 1:2])
+        hidden = jnp.concatenate(
+            [
+                gelu(dot(firstb, wu[l, :, c : c + 256])).astype(jnp.bfloat16)
+                for c in range(0, 2048, 256)
+            ],
+            axis=1,
+        )
+        second = first + normed(dot(hidden, wd[l]), gains[l, 1:2])
         s = l // 2
         applied = lax.rem(l, 2) < depth_ref[chip * 2 + s]
         fresh = jnp.where(applied, second, state)
@@ -454,7 +459,6 @@
             pltpu.VMEM((2, WIDE, width), bf16),
             pltpu.VMEM((2, 2 * EDGE, width), bf16),
             pltpu.VMEM((2, WIDE, width), bf16),
-            pltpu.VMEM((CELLS, 4 * width), bf16),
             pltpu.VMEM((2, 2, CELLS, width), f32),
             pltpu.VMEM((2, CELLS, width), bf16),
             pltpu.VMEM((2, CELLS, width), bf16),

time: 205 us -> 202 us (0.985)
  Pallas kernels: 199 us -> 196 us
    pallas_call x1, Pallas kernels: 199 us -> 196 us  [shards(): pl.pallas_call(functools.partial(kernel, lon_n, lat_n), out_shape=jax.Sha...]
where the time goes in v3:
time: 202 us
  Pallas kernels  196 us (97%)
  local copies, waits for them, and re-layouts  3.42 us (2%)
    pallas_call x1, Pallas kernels, shards(): pl.pallas_call(functools.partial(kernel, lon_n, lat_n), out_shape=jax.Sha...  196 us

profile of v3, /device:TPU:33, one launch (start us, length us, event | category | flops | bytes accessed | tf_op | source)
XLA Modules:
  0.0 201.5 jit_solution(8361715837903190620)
XLA Ops:
  0.0 0.1 pad.2.clone
  0.1 0.7 convert_element_type.3
  0.8 0.7 broadcast_multiply_fusion
  1.4 0.6 maximum_maximum_fusion
  2.1 196.1 %shard_map.100 = f32[4,288,512]{2,1,0:T(8,128)} custom-call(s32[4]{0:T(128)} %depth_ref.1, bf16[4,288,512]{2,1,0:T(8,128)(2,1)} %bitcast.5, f32[2,1,128]{2,1,0:T(1,128)} %bitcast.4, f32[2,2,512]{2,1,0:T(2,128)} %gains_in.1, f32[288,128]{1,0:T(8,128)} %constant.6.clone.table, bf16[2,512,1536]{2,1,0:T(8,128)(2,1)} %w_qkv.1, bf16[2,512,512]{2,1,0:T(8,128)(2,1)} %w_out.1, ...), custom_call_target="tpu_custom_call" | custom-call | flops 32000000000 | bytes 20000000 | tf_op jit(solution)/shard_map/pallas_call | solution.py:441
  198.2 3.3 %copy.12 = f32[1,4,2,6,24,512]{5,4,3,2,1,0:T(8,128)} copy(f32[1,4,2,6,24,512]{5,4,3,2,1,0:T(8,128)} %bitcast.3) | data formatting | bytes 4718592
  (1 shorter events, 0.0 us)
